TPU v7x, 32 devices: a whole 2x2x4 slice. The times are simulated.
32 devices in a mesh: groups: 2 (over y), ffn: 4 (over x, core), hid: 4 (over z).
Axes of the slice: x: 2, y: 2, z: 4, core: 2. Of those that a mesh axis runs over, the one named last changes fastest.
Arguments:
- inputs: bfloat16 [512, 2, 8192], P(('groups', 'ffn'), None, 'hid'), parts along dimension 0, may hold values from -6 to 6
- gate_weight: bfloat16 [8192, 26624], P('hid', 'ffn'), may hold values from -0.0625 to 0.0625
- up_weight: bfloat16 [8192, 26624], P('hid', 'ffn'), may hold values from -0.0625 to 0.0625
- down_weight: bfloat16 [26624, 8192], P('ffn', 'hid'), may hold values from -0.0390625 to 0.0390625
Outputs:
- outputs: bfloat16 [512, 2, 8192], P(('groups', 'ffn'), None, 'hid'), parts along dimension 0
There are 2 independent parts, one for each index of `groups`. A program takes and returns all parts, laid end to end along the dimension named above; an argument that names none is the same for every part. Nothing has to cross between parts.
All inputs are finite; a program needn't handle non-finite values.
Results may differ from a plain program's by a relative error of at most 0.005.
Values may be sent and summed in bfloat16 or wider, within the bound.
A program may use at most 256 MiB of HBM per device.

v0:
```python
import jax
import jax.numpy as jnp
from jax import lax
from jax.sharding import PartitionSpec as P


def per_device(inputs, gate_weight, up_weight, down_weight):
    local_units = gate_weight.shape[1]
    panel = lax.all_gather(inputs, "ffn", axis=0, tiled=True)
    gate_part = jnp.einsum("rsd,df->rsf", panel, gate_weight, preferred_element_type=jnp.float32)
    up_part = jnp.einsum("rsd,df->rsf", panel, up_weight, preferred_element_type=jnp.float32)
    partial_value = jnp.concatenate((gate_part, up_part), axis=2)
    totals = lax.psum(partial_value, "hid")
    hidden = (jax.nn.silu(totals[:, :, :local_units]) * totals[:, :, local_units:]).astype(
        jnp.bfloat16
    )
    result = lax.psum_scatter(
        jnp.einsum("rsf,fd->rsd", hidden, down_weight, preferred_element_type=jnp.float32),
        "ffn",
        scatter_dimension=0,
        tiled=True,
    )
    return result.astype(jnp.bfloat16)


def solution(mesh):
    return jax.shard_map(
        per_device,
        mesh=mesh,
        in_specs=(
            P(("groups", "ffn"), None, "hid"),
            P("hid", "ffn"),
            P("hid", "ffn"),
            P("ffn", "hid"),
        ),
        out_specs=P(("groups", "ffn"), None, "hid"),
        check_vma=False,
    )
```

profile of v0, /device:TPU:1, one launch (start us, length us, event | category | flops | bytes accessed | tf_op | source)
XLA Modules:
  0.0 1084.3 jit_solution(464392651800453892)
XLA Ops:
  6.5 0.0 all-gather.2.cloned.1.call-start
  6.5 2.0 copy.5
  8.5 0.0 all-gather.2.cloned.1.call-update
  8.6 0.0 all-reduce.2.cloned.1.call-start
  8.6 25.4 %all-gather.2.cloned.1.call-done = bf16[256,2,2048]{2,0,1:T(8,128)(2,1)} async-done(((bf16[64,2,2048]{2,0,1:T(8,128)(2,1)}), bf16[256,2,2048]{2,0,1:T(8,128)(2,1)}) %all-gather.2.cloned.1.call-update) | async-done | bytes 2097168 | tf_op jit(solution)/shard_map/all_gather | solution.py:9
  34.0 0.0 copy-start
  34.0 26.3 %fusion.2 = f32[256,2,6656]{2,0,1:T(8,128)} fusion(bf16[256,2,2048]{2,0,1:T(8,128)(2,1)} %all-gather.2.cloned.1.call-done, bf16[2048,6656]{1,0:T(8,128)(2,1)} %param.6), kind=kOutput, calls=%fused_computation.3 | convolution fusion | flops 13958643712 | bytes 42991616 | tf_op jit(solution)/shard_map/rsd,df->rsf/dot_general | solution.py:11
  60.3 0.0 copy-done
  60.3 22.2 %fusion.4 = f32[256,2,6656]{2,0,1:T(8,128)} fusion(bf16[256,2,2048]{2,0,1:T(8,128)(2,1)S(1)} %copy-done, bf16[2048,6656]{1,0:T(8,128)(2,1)} %param.5), kind=kOutput, calls=%fused_computation.5 | convolution fusion | flops 13958643712 | bytes 42991616 | tf_op jit(solution)/shard_map/rsd,df->rsf/dot_general | solution.py:10
  82.6 19.5 %pad_maximum_fusion = f32[256,2,13312]{2,0,1:T(8,128)} fusion(f32[256,2,6656]{2,0,1:T(8,128)} %fusion.2, f32[256,2,6656]{2,0,1:T(8,128)} %fusion.4), kind=kLoop, calls=%fused_computation | loop fusion | flops 6815744 | bytes 54525952 | tf_op jit(solution)/shard_map/concatenate | solution.py:12
  102.1 0.0 all-reduce.2.cloned.1.call-update
  102.1 0.2 reduce-scatter.2.cloned.1.call-start
  102.3 899.7 %all-reduce.2.cloned.1.call-done = f32[256,2,13312]{2,0,1:T(8,128)} async-done(((f32[256,2,13312]{2,0,1:T(8,128)}), f32[256,2,13312]{2,0,1:T(8,128)}) %all-reduce.2.cloned.1.call-update) | async-done | bytes 27262992 | tf_op jit(solution)/shard_map/psum | solution.py:13
  1002.1 29.4 %fusion = f32[256,2,2048]{2,0,1:T(8,128)} fusion(bf16[6656,2048]{1,0:T(8,128)(2,1)} %param.7, f32[256,2,13312]{2,0,1:T(8,128)} %all-reduce.2.cloned.1.call-done), kind=kOutput, calls=%fused_computation.1 | convolution fusion | flops 13979090944 | bytes 58720256 | tf_op jit(solution)/shard_map/rsf,fd->rsd/dot_general | solution.py:18
  1031.5 0.0 reduce-scatter.2.cloned.1.call-update
  1031.5 43.6 %reduce-scatter.2.cloned.1.call-done = f32[64,2,2048]{2,0,1:T(8,128)} async-done(((f32[256,2,2048]{2,0,1:T(8,128)}), f32[64,2,2048]{2,0,1:T(8,128)}) %reduce-scatter.2.cloned.1.call-update) | async-done | bytes 1048592 | tf_op jit(solution)/shard_map/reduce_scatter | solution.py:17
  1075.1 1.3 convert_element_type.7
  1076.4 1.3 copy.6
Async XLA Ops:
  6.5 27.5 %all-gather.2.cloned.1.call-start = ((), (), s32[]{:S(2)}) async-start(), calls=%async_computation.1 | async-start | bytes 2621440 | tf_op jit(solution)/shard_map/all_gather | solution.py:9
  8.6 993.5 %all-reduce.2.cloned.1.call-start = ((), (), s32[]{:S(2)}) async-start(), calls=%async_computation.2 | async-start | bytes 54525952 | tf_op jit(solution)/shard_map/psum | solution.py:13
  34.0 26.3 %copy-start = (bf16[256,2,2048]{2,0,1:T(8,128)(2,1)S(1)}, bf16[256,2,2048]{2,0,1:T(8,128)(2,1)}, u32[]{:S(2)}) copy-start(bf16[256,2,2048]{2,0,1:T(8,128)(2,1)} %all-gather.2.cloned.1.call-done) | copy-start | bytes 6291460
  102.1 973.0 %reduce-scatter.2.cloned.1.call-start = ((), (), s32[]{:S(2)}) async-start(), calls=%async_computation.3 | async-start | bytes 5242880 | tf_op jit(solution)/shard_map/reduce_scatter | solution.py:17
Sparse Core Ops, SparseCore 0:
  8.9 25.0 all-gather.1
  102.2 899.7 all-reduce.1
  1031.7 43.3 reduce-scatter.1
where the time goes:
time: 1090 us; the launch traced here: 1080 us
  waiting for transfers between devices  969 us (89%)
  matrix products  78 us (7%)
  other arithmetic  20.8 us (2%)
  between operations  13.1 us (1%)
    psum x1, waiting for transfers between devices, per_device(): totals = lax.psum(partial_value, 'hid')  900 us
    reduce_scatter x1, waiting for transfers between devices, per_device(): lax.psum_scatter(jnp.einsum('rsf,fd->rsd', hidden, down_weight, preferred...  43.6 us
    dot_general x1, matrix products, per_device(): jnp.einsum('rsf,fd->rsd', hidden, down_weight, preferred_element_type=jnp...  29.4 us
    dot_general x1, matrix products, per_device(): jnp.einsum('rsd,df->rsf', panel, up_weight, preferred_element_type=jnp.fl...  26.3 us
    all_gather x1, waiting for transfers between devices, per_device(): panel = lax.all_gather(inputs, 'ffn', axis=0, tiled=True)  25.4 us
    dot_general x1, matrix products, per_device(): jnp.einsum('rsd,df->rsf', panel, gate_weight, preferred_element_type=jnp....  22.2 us
  transfers between devices with their start and end apart: 3, of which 3 were waited for; matrix products, arithmetic and copies ran while one was open for 0% of the time, Pallas kernels for 0%

commit v1 on v0

v1 whole, which is shorter than its diff:
```python
import functools

import jax
import jax.numpy as jnp
from jax import lax
from jax.experimental import pallas as pl
from jax.experimental.pallas import tpu as pltpu
from jax.sharding import PartitionSpec as P

MESH = pl.DeviceIdType.MESH
GROUPS_OF_ROWS = 2
LAG = 2


def remote(src, dst, send_sem, recv_sem, device_id):
    return pltpu.make_async_remote_copy(
        src_ref=src,
        dst_ref=dst,
        send_sem=send_sem,
        recv_sem=recv_sem,
        device_id=device_id,
        device_id_type=MESH,
    )


def kernel(
    nf, nz, chunk,
    x_ref, wg_ref, wu_ref, wd_ref, out_ref,
    panel, wbuf, dbuf, ring, buf, hid, acc, rs1, snd2, rs2,
    w_sem, d_sem, ps_sem, pr_sem, hs_sem, hr_sem,
    gx_s, gx_r, gc_s, gc_r, c_s, c_r, o_s, o_r,
):
    ng, rg, k = x_ref.shape
    nx = nf // 2
    half = nf // 2
    rows = half * rg
    chunks = wg_ref.shape[1] // chunk
    steps = ng * chunks
    slots = ring.shape[0]

    z = lax.axis_index("hid")
    me = lax.axis_index("ffn")
    x = lax.div(me, 2)
    c = lax.rem(me, 2)
    sibling = {"ffn": 2 * x + 1 - c}

    def ahead(o):
        return lax.rem(x + o, nx)

    def behind(o):
        return lax.rem(x + nx - o, nx)

    def fetch_w(u, action):
        col = pl.ds(pl.multiple_of(lax.rem(u, chunks) * chunk, chunk), chunk)
        slot = lax.rem(u, 2)
        for n, ref in enumerate((wg_ref, wu_ref)):
            action(pltpu.make_async_copy(ref.at[:, col], wbuf.at[slot, n], w_sem.at[slot, n]))

    def fetch_d(way, s, action):
        row = pl.ds(pl.multiple_of(lax.rem(s, chunks) * chunk, chunk), chunk)
        slot = lax.rem(s, 2)
        action(pltpu.make_async_copy(wd_ref.at[row, :], dbuf.at[way, slot], d_sem.at[way, slot]))

    def start(copy):
        copy.start()

    def wait(copy):
        copy.wait()

    fetch_w(jnp.int32(0), start)
    fetch_w(jnp.int32(1), start)

    barrier = pltpu.get_barrier_semaphore()
    pl.semaphore_signal(barrier, inc=1, device_id=sibling, device_id_type=MESH)
    for o in range(1, nx):
        pl.semaphore_signal(
            barrier, inc=1, device_id={"ffn": 2 * ahead(o) + c}, device_id_type=MESH
        )

    @pl.when(z > 0)
    def _():
        pl.semaphore_signal(barrier, inc=1, device_id={"hid": z - 1}, device_id_type=MESH)

    @pl.when(z < nz - 1)
    def _():
        pl.semaphore_signal(barrier, inc=1, device_id={"hid": z + 1}, device_id_type=MESH)

    inner = jnp.where(jnp.logical_and(z > 0, z < nz - 1), 1, 0)
    pl.semaphore_wait(barrier, nx + 1 + inner)

    def to_peer(g, o):
        return remote(
            x_ref.at[g], panel.at[g, me], gx_s.at[g, o], gx_r.at[g, o],
            {"ffn": 2 * ahead(o) + c},
        )

    def from_peer(g, o):
        block = panel.at[g, 2 * behind(o) + c]
        return remote(block, block, gx_s.at[g, o], gx_r.at[g, o], sibling)

    def to_sibling(g, o):
        block = panel.at[g, 2 * behind(o) + c]
        return remote(
            x_ref.at[g] if o == 0 else block, block, gc_s.at[g, o], gc_r.at[g, o], sibling
        )

    def from_sibling(g, o):
        block = panel.at[g, 2 * behind(o) + 1 - c]
        return remote(block, block, gc_s.at[g, o], gc_r.at[g, o], sibling)

    def gather_start(g):
        for o in range(1, nx):
            to_peer(g, o).start()
        to_sibling(g, 0).start()
        panel[g, me] = x_ref[g]

    def gather_forward(g):
        for o in range(1, nx):
            from_peer(g, o).wait_recv()
            to_sibling(g, o).start()

    def gather_end(g):
        for o in range(nx):
            from_sibling(g, o).wait_recv()
        for o in range(1, nx):
            to_peer(g, o).wait_send()
        for o in range(nx):
            to_sibling(g, o).wait_send()

    def to_core(g, p):
        return remote(
            acc.at[g, 2 * p + 1 - c], rs1.at[g, p], c_s.at[g, p], c_r.at[g, p], sibling
        )

    def to_chip(g, o):
        return remote(
            snd2.at[g, o - 1], rs2.at[g, o - 1], o_s.at[g, o], o_r.at[g, o],
            {"ffn": 2 * ahead(o) + c},
        )

    def reduce_start(g):
        for p in range(nx):
            to_core(g, p).start()

    def reduce_middle(g):
        for p in range(nx):
            to_core(g, p).wait_recv()
        for o in range(1, nx):
            p = ahead(o)
            snd2[g, o - 1] = (acc[g, 2 * p + c] + rs1[g, p]).astype(jnp.bfloat16)
            to_chip(g, o).start()

    def reduce_end(g):
        total = acc[g, me] + rs1[g, x]
        for o in range(1, nx):
            to_chip(g, o).wait_recv()
            total = total + rs2[g, o - 1].astype(jnp.float32)
        out_ref[g] = total.astype(jnp.bfloat16)
        for p in range(nx):
            to_core(g, p).wait_send()
        for o in range(1, nx):
            to_chip(g, o).wait_send()

    def project(u):
        g = lax.div(u, chunks)
        slot = lax.rem(u, 2)
        at = lax.rem(u, slots)
        fetch_w(u, wait)
        left = panel[g].reshape(nf * rg, k)
        for n in range(2):
            part = jnp.dot(left, wbuf[slot, n], preferred_element_type=jnp.float32)
            ring[at, 0, :, n * chunk:(n + 1) * chunk] = part[:rows]
            ring[at, 1, :, n * chunk:(n + 1) * chunk] = part[rows:]

    ways = []
    for way in range(2):
        place = z if way == 1 else nz - 1 - z
        sign = 1 if way == 1 else -1
        ways.append((place, {"hid": z + sign}, {"hid": z - sign}))

    def send_sum(way, s, device):
        block = buf.at[way, s]
        return remote(block, block, ps_sem.at[way, s], pr_sem.at[way, s], device)

    def send_hid(way, s, device):
        block = hid.at[way, s]
        return remote(block, block, hs_sem.at[way, s], hr_sem.at[way, s], device)

    def combine(way, t):
        place, onward, back = ways[way]
        s = t - LAG * place

        @pl.when(jnp.logical_and(s >= 0, s < steps))
        def _():
            at = lax.rem(s, slots)

            @pl.when(place == 0)
            def _():
                buf[way, s] = ring[at, way].astype(jnp.bfloat16)
                send_sum(way, s, onward).start()

            @pl.when(jnp.logical_and(place > 0, place < nz - 1))
            def _():
                send_sum(way, s, back).wait_recv()
                buf[way, s] = (buf[way, s].astype(jnp.float32) + ring[at, way]).astype(
                    jnp.bfloat16
                )
                send_sum(way, s, onward).start()

            @pl.when(place == nz - 1)
            def _():
                send_sum(way, s, back).wait_recv()
                total = buf[way, s].astype(jnp.float32) + ring[at, way]
                gate = total[:, :chunk]
                up = total[:, chunk:]
                hid[way, s] = (gate / (1.0 + jnp.exp(-gate)) * up).astype(jnp.bfloat16)
                send_hid(way, s, back).start()

    def step_of(way, t):
        return t - LAG * (2 * (nz - 1) - ways[way][0])

    def forward(way, t):
        place, onward, back = ways[way]
        s = step_of(way, t)

        @pl.when(jnp.logical_and(jnp.logical_and(s >= 0, s < steps), place < nz - 1))
        def _():
            send_hid(way, s, onward).wait_recv()

            @pl.when(place > 0)
            def _():
                send_hid(way, s, back).start()

    def down(way, t):
        s = step_of(way, t)

        @pl.when(jnp.logical_and(s + 1 >= 0, s + 1 < steps))
        def _():
            fetch_d(way, s + 1, start)

        @pl.when(jnp.logical_and(s >= 0, s < steps))
        def _():
            g = lax.div(s, chunks)
            fetch_d(way, s, wait)
            part = jnp.dot(
                hid[way, s], dbuf[way, lax.rem(s, 2)], preferred_element_type=jnp.float32
            )
            blocks = pl.ds(way * half, half)
            acc[g, blocks] += part.reshape(half, rg, part.shape[1])

    gather_start(0)
    acc[...] = jnp.zeros_like(acc)
    gather_forward(0)
    gather_end(0)
    project(jnp.int32(0))

    drain = LAG * 2 * (nz - 1)

    def body(t, carry):
        for way in range(2):
            combine(way, t)
        for way in range(2):
            forward(way, t)

        @pl.when(t + 2 < steps)
        def _():
            fetch_w(t + 2, start)

        for g in range(1, ng):
            @pl.when(t == (g - 1) * chunks + 2)
            def _():
                gather_start(g)

            @pl.when(t == g * chunks - 3)
            def _():
                gather_forward(g)

            @pl.when(t == g * chunks - 1)
            def _():
                gather_end(g)

        @pl.when(t + 1 < steps)
        def _():
            project(t + 1)

        for way in range(2):
            down(way, t)

        for g in range(ng - 1):
            done = (g + 1) * chunks - 1 + drain

            @pl.when(t == done)
            def _():
                reduce_start(g)

            @pl.when(t == done + 2)
            def _():
                reduce_middle(g)

            @pl.when(t == done + 5)
            def _():
                reduce_end(g)

        return carry

    lax.fori_loop(0, steps + drain, body, 0)

    last = ng - 1
    reduce_start(last)
    reduce_middle(last)
    reduce_end(last)

    def finish(s, carry):
        for way in range(2):
            place, onward, back = ways[way]

            @pl.when(place < nz - 1)
            def _():
                send_sum(way, s, onward).wait_send()

            @pl.when(place > 0)
            def _():
                send_hid(way, s, back).wait_send()

        return carry

    lax.fori_loop(0, steps, finish, 0)


def per_device(nf, nz, inputs, gate_weight, up_weight, down_weight):
    ng = GROUPS_OF_ROWS
    k = inputs.shape[2]
    block = inputs.shape[0] * inputs.shape[1]
    rg = block // ng
    nx = nf // 2
    rows = nx * rg
    units = gate_weight.shape[1]
    chunk = 256 if units % 256 == 0 else 128
    steps = ng * (units // chunk)
    slots = LAG * (nz - 1) + 1
    wide = down_weight.shape[1]
    bf16, f32 = jnp.bfloat16, jnp.float32
    dma = pltpu.SemaphoreType.DMA
    peers = max(nx - 1, 1)
    result = pl.pallas_call(
        functools.partial(kernel, nf, nz, chunk),
        out_shape=jax.ShapeDtypeStruct((ng, rg, wide), bf16),
        in_specs=[pl.BlockSpec(memory_space=pltpu.VMEM)]
        + [pl.BlockSpec(memory_space=pl.ANY)] * 3,
        out_specs=pl.BlockSpec(memory_space=pltpu.VMEM),
        scratch_shapes=[
            pltpu.VMEM((ng, nf, rg, k), bf16),
            pltpu.VMEM((2, 2, k, chunk), bf16),
            pltpu.VMEM((2, 2, chunk, wide), bf16),
            pltpu.VMEM((slots, 2, rows, 2 * chunk), f32),
            pltpu.VMEM((2, steps, rows, 2 * chunk), bf16),
            pltpu.VMEM((2, steps, rows, chunk), bf16),
            pltpu.VMEM((ng, nf, rg, wide), f32),
            pltpu.VMEM((ng, nx, rg, wide), f32),
            pltpu.VMEM((ng, peers, rg, wide), bf16),
            pltpu.VMEM((ng, peers, rg, wide), bf16),
            dma((2, 2)),
            dma((2, 2)),
            dma((2, steps)),
            dma((2, steps)),
            dma((2, steps)),
            dma((2, steps)),
            dma((ng, nx)),
            dma((ng, nx)),
            dma((ng, nx)),
            dma((ng, nx)),
            dma((ng, nx)),
            dma((ng, nx)),
            dma((ng, nx)),
            dma((ng, nx)),
        ],
        compiler_params=pltpu.CompilerParams(
            collective_id=0, has_side_effects=True, vmem_limit_bytes=60 * 1024 * 1024
        ),
    )(inputs.reshape(ng, rg, k), gate_weight, up_weight, down_weight)
    return result.reshape(inputs.shape[0], inputs.shape[1], wide)


def solution(mesh):
    return jax.shard_map(
        functools.partial(per_device, mesh.shape["ffn"], mesh.shape["hid"]),
        mesh=mesh,
        in_specs=(
            P(("groups", "ffn"), None, "hid"),
            P("hid", "ffn"),
            P("hid", "ffn"),
            P("ffn", "hid"),
        ),
        out_specs=P(("groups", "ffn"), None, "hid"),
        check_vma=False,
    )
```

time: 1090 us -> 268 us (0.25)
  waiting for transfers between devices: 969 us -> 0 us
  Pallas kernels: 0 us -> 263 us
  matrix products: 78 us -> 0 us
  other arithmetic: 20.8 us -> 0 us
  between operations: 13.1 us -> 0.01 us
    psum x1 -> x0, waiting for transfers between devices: 900 us -> none  [per_device(): totals = lax.psum(partial_value, 'hid')]
    pallas_call x0 -> x1, Pallas kernels: none -> 263 us  [per_device(): pl.pallas_call(functools.partial(kernel, nf, nz, chunk), out_shape=jax.Sh...]
    dot_general x3 -> x0, matrix products: 78 us -> none  [the longest x1 29.4 us: per_device(): jnp.einsum('rsf,fd->rsd', hidden, down_weight, preferred_element_type=jnp...]
    reduce_scatter x1 -> x0, waiting for transfers between devices: 43.6 us -> none  [per_device(): lax.psum_scatter(jnp.einsum('rsf,fd->rsd', hidden, down_weight, preferred...]
    all_gather x1 -> x0, waiting for transfers between devices: 25.4 us -> none  [per_device(): panel = lax.all_gather(inputs, 'ffn', axis=0, tiled=True)]
    concatenate x1 -> x0, other arithmetic: 19.5 us -> none  [per_device(): partial_value = jnp.concatenate((gate_part, up_part), axis=2)]
  transfers between devices with their start and end apart: 3 -> 0, of which waited for: 3 -> 0; matrix products, arithmetic and copies ran while one was open for 0% -> 0% of each run, Pallas kernels for 0% -> 0%
where the time goes in v1:
time: 268 us
  Pallas kernels  263 us (98%)
  local copies, waits for them, and re-layouts  4.2 us (2%)
    pallas_call x1, Pallas kernels, per_device(): pl.pallas_call(functools.partial(kernel, nf, nz, chunk), out_shape=jax.Sh...  263 us

profile of v1, /device:TPU:1, one launch (start us, length us, event | category | flops | bytes accessed | tf_op | source)
XLA Modules:
  0.0 267.7 jit_solution(1985893396842404015)
XLA Ops:
  0.0 2.0 reshape.6.x_ref
  2.0 263.5 %shard_map.46 = bf16[2,64,2048]{2,1,0:T(8,128)(2,1)} custom-call(bf16[2,64,2048]{2,1,0:T(8,128)(2,1)} %reshape.6.x_ref, bf16[2048,6656]{1,0:T(8,128)(2,1)} %wg_ref.1, bf16[2048,6656]{1,0:T(8,128)(2,1)} %wu_ref.1, bf16[6656,2048]{1,0:T(8,128)(2,1)} %wd_ref.1), custom_call_target="tpu_custom_call" | custom-call | tf_op jit(solution)/shard_map/pallas_call | solution.py:345
  265.5 2.2 reshape.7

commit v2 on v1

--- a/solution.py
+++ b/solution.py
@@ -9,7 +9,7 @@
 
 MESH = pl.DeviceIdType.MESH
 GROUPS_OF_ROWS = 2
-LAG = 2
+LAG = 1
 
 
 def remote(src, dst, send_sem, recv_sem, device_id):

time: 268 us -> 298 us (1.11)
  Pallas kernels: 263 us -> 293 us
    pallas_call x1, Pallas kernels: 263 us -> 293 us  [per_device(): pl.pallas_call(functools.partial(kernel, nf, nz, chunk), out_shape=jax.Sh...]
where the time goes in v2:
time: 298 us; the launch traced here: 297 us
  Pallas kernels  293 us (98%)
  local copies, waits for them, and re-layouts  4.2 us (1%)
    pallas_call x1, Pallas kernels, per_device(): pl.pallas_call(functools.partial(kernel, nf, nz, chunk), out_shape=jax.Sh...  293 us

profile of v2, /device:TPU:1, one launch (start us, length us, event | category | flops | bytes accessed | tf_op | source)
XLA Modules:
  0.0 297.4 jit_solution(15760950250068171955)
XLA Ops:
  0.0 2.0 reshape.6.x_ref
  2.0 293.2 %shard_map.46 = bf16[2,64,2048]{2,1,0:T(8,128)(2,1)} custom-call(bf16[2,64,2048]{2,1,0:T(8,128)(2,1)} %reshape.6.x_ref, bf16[2048,6656]{1,0:T(8,128)(2,1)} %wg_ref.1, bf16[2048,6656]{1,0:T(8,128)(2,1)} %wu_ref.1, bf16[6656,2048]{1,0:T(8,128)(2,1)} %wd_ref.1), custom_call_target="tpu_custom_call" | custom-call | tf_op jit(solution)/shard_map/pallas_call | solution.py:345
  295.2 2.2 reshape.7
